TPU v7x, 768 devices: a whole 4x8x12 slice. The times are simulated.
768 devices in a mesh: dp: 192 (over z, y, core), expert: 4 (over x).
Axes of the slice: x: 4, y: 8, z: 12, core: 2. Of those that a mesh axis runs over, the one named last changes fastest.
Arguments:
- gate_pre: bfloat16 [49152, 1024], P('dp', 'expert'), may hold values from -6 to 6
- up_pre: bfloat16 [49152, 1024], P('dp', 'expert'), may hold values from -6 to 6
- out_grad: bfloat16 [49152, 3840], P('dp'), may hold values from -24 to 24
- route_weight: float32 [49152], P('dp'), may hold values from 0.05 to 0.6
- counts: int32 [192], P('dp'), may hold values from 32 to 256, as said below
- down_weight: bfloat16 [3840, 1024], P('dp', 'expert'), may hold values from -0.1875 to 0.1875
Outputs:
- gate_grad: bfloat16 [49152, 1024], P('dp', 'expert')
- up_grad: bfloat16 [49152, 1024], P('dp', 'expert')
- route_grad: float32 [49152], P('dp')
- down_grad: float32 [3840, 1024], P('dp', 'expert')
Inputs may be any that keep to these rules, and one draw needn't show every extreme that they name: The live rows of data shard i are its first counts[i] slots; some shard is full and some holds the fewest.
All inputs are finite; a program needn't handle non-finite values.
Results may differ from a plain program's by a relative error of at most 0.007.
Values may be sent and summed in bfloat16 or wider, within the bound.
A program may use at most 32 MiB of HBM per device.

v0:
```python
import math

import jax
import jax.numpy as jnp
from jax import lax
from jax.sharding import PartitionSpec as P


def on_device(gate_pre, up_pre, out_grad, route_weight, counts, down_weight):
    row_count = gate_pre.shape[0]
    grad_norm = 1.0 / math.sqrt(row_count * lax.axis_size("dp"))
    slot_index = lax.iota(jnp.int32, row_count)
    live_mask = (slot_index < counts[0]).astype(jnp.float32)
    row_scale = route_weight * live_mask
    gate_wide = gate_pre.astype(jnp.float32)
    up_wide = up_pre.astype(jnp.float32)
    sigmoid_gate = jax.nn.sigmoid(gate_wide)
    activated = gate_wide * sigmoid_gate
    hidden = (activated * up_wide).astype(jnp.bfloat16)
    gathered = lax.all_gather(down_weight, "dp", axis=0, tiled=True)
    back_proj = jnp.dot(out_grad, gathered, preferred_element_type=jnp.float32)
    hid_grad = back_proj * row_scale[:, None]
    gate_grad = (
        hid_grad * up_wide * sigmoid_gate * (1.0 + gate_wide * (1.0 - sigmoid_gate))
    ).astype(jnp.bfloat16)
    up_grad = (hid_grad * activated).astype(jnp.bfloat16)
    partial_match = jnp.sum(hidden.astype(jnp.float32) * back_proj, axis=1)
    route_grad = lax.psum(partial_match, "expert") * live_mask
    scaled = (out_grad.astype(jnp.float32) * row_scale[:, None]).astype(jnp.bfloat16)
    half_width = hidden.shape[1] // 2
    halves = []
    for half_index in range(2):
        hidden_half = hidden[:, half_index * half_width : (half_index + 1) * half_width]
        product = lax.dot_general(
            scaled, hidden_half, (((0,), (0,)), ((), ())), preferred_element_type=jnp.float32
        )
        halves.append(lax.psum_scatter(product * grad_norm, "dp", scatter_dimension=0, tiled=True))
    down_grad = jnp.concatenate(halves, axis=1)
    return (gate_grad, up_grad, route_grad, down_grad)


def solution(mesh):
    return jax.shard_map(
        on_device,
        mesh=mesh,
        in_specs=(
            P("dp", "expert"),
            P("dp", "expert"),
            P("dp", None),
            P("dp"),
            P("dp"),
            P("dp", "expert"),
        ),
        out_specs=(P("dp", "expert"), P("dp", "expert"), P("dp"), P("dp", "expert")),
        check_vma=False,
    )
```

profile of v0, /device:TPU:1, one launch (start us, length us, event | category | flops | bytes accessed | tf_op | source)
XLA Modules:
  0.0 488.6 jit_solution(4859106583533987443)
XLA Ops:
  7.2 0.0 all-gather.3.cloned.1.call-start
  7.2 0.7 all-gather.3.cloned.1.call-update
  7.9 0.0 all-reduce.5.cloned.1.call-start
  7.9 1.0 copy.18
  9.0 1.0 copy.19
  10.6 0.7 fusion.11
  11.3 0.0 copy-start
  11.3 130.6 %all-gather.3.cloned.1.call-done = bf16[192,20,256]{2,1,0:T(8,128)(2,1)} async-done(((bf16[1,20,256]{2,1,0:T(8,128)(2,1)}), bf16[192,20,256]{2,1,0:T(8,128)(2,1)}) %all-gather.3.cloned.1.call-update) | async-done | bytes 1966096 | tf_op jit(solution)/shard_map/all_gather | solution.py:20
  141.9 3.9 reshape.10
  145.8 0.0 copy-done
  145.8 2.5 multiply_reduce_fusion
  148.3 2.1 convolution_multiply_fusion
  150.4 2.1 convolution_multiply_fusion.1
  152.5 0.0 all-reduce.5.cloned.1.call-update
  152.6 1.3 dynamic-slice
  154.5 0.8 copy.20
  155.3 0.8 copy.21
  156.0 8.4 %psum.7 = f32[256]{0:T(256)S(1)} all-reduce(f32[256]{0:T(256)S(1)} %get-tuple-element.18), channel_id=1, replica_groups=mesh['dp'=192,'expert'=4] {'expert'}, use_global_device_ids=true, to_apply=%region_1.0 | all-reduce | flops 256 | bytes 2048 | tf_op jit(solution)/shard_map/psum | solution.py:28
  164.4 0.6 fusion.10
  165.0 315.4 %all-reduce.5.cloned.1.call-done = (f32[3840,128]{1,0:T(8,128)}, f32[3840,128]{1,0:T(8,128)}) async-done(((f32[3840,128]{1,0:T(8,128)}, f32[3840,128]{1,0:T(8,128)}), (f32[3840,128]{1,0:T(8,128)}, f32[3840,128]{1,0:T(8,128)})) %all-reduce.5.cloned.1.call-update) | async-done | bytes 3932176
  480.4 0.7 constant_dynamic-slice_fusion
  481.1 0.6 pad_maximum_fusion
Async XLA Ops:
  7.2 134.7 %all-gather.3.cloned.1.call-start = ((), (), s32[]{:S(2)}) async-start(), calls=%async_computation | async-start | bytes 2371584 | tf_op jit(solution)/shard_map/all_gather | solution.py:20
  7.9 472.5 %all-reduce.5.cloned.1.call-start = ((), (), s32[]{:S(2)}) async-start(), calls=%async_computation.1 | async-start | bytes 7864320
  11.3 134.5 %copy-start = (bf16[256,3840]{1,0:T(8,128)(2,1)S(1)}, bf16[256,3840]{1,0:T(8,128)(2,1)}, u32[]{:S(2)}) copy-start(bf16[256,3840]{1,0:T(8,128)(2,1)} %param.8) | copy-start | bytes 5898244
Sparse Core Ops, SparseCore 0:
  11.8 130.0 all-gather.2
  152.7 327.6 all-reduce.4
where the time goes:
time: 490 us; the launch traced here: 489 us
  waiting for transfers between devices  447 us (91%)
  between operations  15.4 us (3%)
  local copies, waits for them, and re-layouts  9.49 us (2%)
  blocking collectives  8.38 us (2%)
  matrix products  6.72 us (1%)
    unnamed x3, waiting for transfers between devices  316 us
    all_gather x1, waiting for transfers between devices, on_device(): gathered = lax.all_gather(down_weight, 'dp', axis=0, tiled=True)  131 us
  transfers between devices with their start and end apart: 2, of which 2 were waited for; matrix products, arithmetic and copies ran while one was open for 1% of the time, Pallas kernels for 0%

commit v1 on v0

v1 whole, which is shorter than its diff:
```python
import math

import jax
import jax.numpy as jnp
from jax import lax
from jax.experimental import pallas as pl
from jax.experimental.pallas import tpu as pltpu
from jax.sharding import PartitionSpec as P

MESH = pl.DeviceIdType.MESH
F32, BF16 = jnp.float32, jnp.bfloat16


def kernel(
    gate_ref, up_ref, og_ref, weight_ref, counts_ref, w_ref,
    gate_out, up_out, route_out, down_out,
    wf, g0_send, g0_recv, far, ybuf, wh, p_own, p_send, p_recv, r1_send, r1_recv,
    t_own, r2_send, r2_recv, u_own, r3_recv, f_send, f_recv, x_send, x_recv,
    hid, gate_co, up_co,
    pair_s, pair_r, far_s, far_r, y_s, y_r, near_s, near_r, fwd_s, fwd_r,
    psum_s, psum_r, r1_s, r1_r, r2_s, r2_r, r3_s, r3_r, x_s, x_r,
):
    me, x = lax.axis_index("dp"), lax.axis_index("expert")
    z, y, c = me // 16, lax.rem(me // 2, 8), lax.rem(me, 2)
    zdiv, zmod = z // 3, lax.rem(z, 3)
    first = c == 0

    def at(dz=0, dy=0, dc=0):
        return {"dp": lax.rem(z + dz, 12) * 16 + lax.rem(y + dy, 8) * 2 + lax.rem(c + dc, 2)}

    def across(k):
        return {"expert": lax.rem(x + k, 4)}

    def send(src, dst, ssem, rsem, device):
        copy = pltpu.make_async_remote_copy(
            src_ref=src, dst_ref=dst, send_sem=ssem, recv_sem=rsem, device_id=device, device_id_type=MESH
        )
        copy.start()
        return copy

    barrier = pltpu.get_barrier_semaphore()
    partners = [at(dc=1)] + [at(dz=d) for d in (1, 11, 3, 6, 9)] + [at(dy=d) for d in range(1, 8)]
    partners += [across(k) for k in range(1, 4)]
    for device in partners:
        pl.semaphore_signal(barrier, inc=1, device_id=device, device_id_type=MESH)

    wf[...] = jnp.zeros_like(wf)
    wf[0:20, :] = w_ref[...].astype(F32)
    g0_recv[24:40, :] = jnp.zeros((16, 128), F32)
    g0_send[...] = jnp.where(first, wf[0:24, 128:256], wf[0:24, 0:128])
    pl.semaphore_wait(barrier, len(partners))
    pair = send(g0_send, g0_recv.at[pl.ds(0, 24)], pair_s.at[0], pair_r.at[0], at(dc=1))

    eye = lax.broadcasted_iota(jnp.int32, (256, 256), 0) == lax.broadcasted_iota(jnp.int32, (256, 256), 1)
    live_row = (lax.broadcasted_iota(jnp.int32, (1, 256), 1) < counts_ref[0]).astype(F32)
    scale_row = weight_ref[...] * live_row
    scale = jnp.sum(jnp.where(eye, jnp.broadcast_to(scale_row, (256, 256)), 0.0), axis=1, keepdims=True)

    pair.wait_recv()
    mine = jnp.where(first, wf[:, 0:128], wf[:, 128:256])
    other = g0_recv[...]
    block = jnp.where(first, mine + pltpu.roll(other, 20, 0), other + pltpu.roll(mine, 20, 0))
    far[zdiv] = jnp.concatenate([block, jnp.zeros((8, 128), F32)], axis=0).astype(BF16)
    fars = [send(far.at[zdiv], far.at[zdiv], far_s.at[k - 1], far_r.at[k - 1], at(dz=3 * k)) for k in (2, 1, 3)]

    gate, up = gate_ref[...].astype(F32), up_ref[...].astype(F32)
    sig = jax.nn.sigmoid(gate)
    act = gate * sig
    hid[...] = (act * up).astype(BF16)
    gate_co[...] = scale * up * sig * (1.0 + gate * (1.0 - sig))
    up_co[...] = scale * act

    psums = []
    for k in range(6):
        scaled = (og_ref[:, 640 * k : 640 * (k + 1)].astype(F32) * scale).astype(BF16)
        part = lax.dot_general(scaled, hid[...], (((0,), (0,)), ((), ())), preferred_element_type=F32)
        lo, hi = part[:, 0:128], part[:, 128:256]
        p_own[2 * k : 2 * k + 2] = jnp.where(first, lo, hi).reshape(2, 320, 128)
        p_send[2 * k : 2 * k + 2] = jnp.where(first, hi, lo).reshape(2, 320, 128).astype(BF16)
        chunk = pl.ds(2 * k, 2)
        psums.append(send(p_send.at[chunk], p_recv.at[chunk], psum_s.at[k], psum_r.at[k], at(dc=1)))

    for copy in fars:
        copy.wait_recv()
    ybuf[y] = jnp.concatenate([far[j].astype(F32)[0:40] for j in range(4)], axis=0).astype(BF16)
    ys = [send(ybuf.at[y], ybuf.at[y], y_s.at[d - 1], y_r.at[d - 1], at(dy=d)) for d in (4, 3, 5, 2, 6, 1, 7)]

    for copy in psums:
        copy.wait_recv()
    r1s = []
    for j in range(4):
        for side, step in enumerate((1, 11)):
            at_z = 3 * j + lax.rem(zmod + step, 3)
            r1_send[side, j] = (p_own[at_z] + p_recv[at_z].astype(F32)).astype(BF16)
            r1s.append(send(r1_send.at[side, j], r1_recv.at[side, j], r1_s.at[side, j], r1_r.at[side, j], at(dz=step)))

    for copy in ys:
        copy.wait_recv()
    for j in range(4):
        rows = [ybuf[i].astype(F32)[40 * j : 40 * j + 40] for i in range(8)]
        wh[c, zmod, j] = jnp.concatenate(rows, axis=0).astype(BF16)
    nears = [
        send(wh.at[c, zmod], wh.at[c, zmod], near_s.at[side], near_r.at[side], at(dz=step))
        for side, step in enumerate((1, 11))
    ]
    fwds = [send(wh.at[c, zmod], wh.at[c, zmod], fwd_s.at[0], fwd_r.at[0], at(dc=1))]

    for copy in r1s:
        copy.wait_recv()
    for j in range(4):
        at_z = 3 * j + zmod
        total = p_own[at_z] + p_recv[at_z].astype(F32) + (r1_recv[0, j].astype(F32) + r1_recv[1, j].astype(F32))
        for i in range(8):
            t_own[i, 40 * j : 40 * j + 40, :] = total[40 * i : 40 * i + 40]
    r2_send[...] = t_own[...].astype(BF16)
    r2s = [
        send(r2_send.at[lax.rem(y + d, 8)], r2_recv.at[d - 1], r2_s.at[d - 1], r2_r.at[d - 1], at(dy=d))
        for d in (4, 3, 5, 2, 6, 1, 7)
    ]

    for side in range(2):
        nears[side].wait_recv()
        m = lax.rem(zmod + 2 - side, 3)
        fwds.append(send(wh.at[c, m], wh.at[c, m], fwd_s.at[side + 1], fwd_r.at[side + 1], at(dc=1)))

    for copy in r2s:
        copy.wait_recv()
    total = t_own[y]
    for d in range(7):
        total = total + r2_recv[d].astype(F32)
    u_own[...] = total.reshape(4, 40, 128)
    r3s = [
        send(u_own.at[lax.rem(zdiv + k, 4)], r3_recv.at[k - 1], r3_s.at[k - 1], r3_r.at[k - 1], at(dz=3 * k))
        for k in (2, 1, 3)
    ]

    for copy in fwds:
        copy.wait_recv()
    proj = None
    for k in range(6):
        halves = []
        for h in range(2):
            blocks = [wh[h, b % 3, b // 3] for b in (2 * k, 2 * k + 1)]
            halves.append(jnp.concatenate(blocks, axis=0))
        term = jnp.dot(
            og_ref[:, 640 * k : 640 * (k + 1)], jnp.concatenate(halves, axis=1), preferred_element_type=F32
        )
        proj = term if proj is None else proj + term
    match = jnp.sum(hid[...].astype(F32) * proj, axis=1, keepdims=True)
    match_row = jnp.sum(jnp.where(eye, jnp.broadcast_to(match, (256, 256)), 0.0), axis=0, keepdims=True)
    x_send[...] = jnp.broadcast_to(match_row, (8, 256))
    xs = [send(x_send, x_recv.at[k - 1], x_s.at[k - 1], x_r.at[k - 1], across(k)) for k in (2, 1, 3)]
    gate_out[...] = (proj * gate_co[...]).astype(BF16)
    up_out[...] = (proj * up_co[...]).astype(BF16)

    for copy in r3s:
        copy.wait_recv()
    total = (u_own[zdiv] + r3_recv[0] + (r3_recv[1] + r3_recv[2])) * (1.0 / math.sqrt(49152))
    turned = pltpu.roll(total, 20, 0)
    f_send[...] = jnp.where(first, turned, total)[0:24]
    final = send(f_send, f_recv, pair_s.at[1], pair_r.at[1], at(dc=1))
    keep = jnp.where(first, total, turned)[0:24]
    final.wait_recv()
    got = f_recv[...]
    down_out[:, 0:128] = jnp.where(first, keep, got)[0:20]
    down_out[:, 128:256] = jnp.where(first, got, keep)[0:20]

    for copy in xs:
        copy.wait_recv()
    everyone = x_send[...] + x_recv[0] + (x_recv[1] + x_recv[2])
    route_out[...] = everyone[0:1] * live_row
    for copy in [pair, final] + fars + ys + nears + fwds + psums + r1s + r2s + r3s + xs:
        copy.wait_send()


def on_device(gate_pre, up_pre, out_grad, route_weight, counts, down_weight):
    vmem = pl.BlockSpec(memory_space=pltpu.VMEM)
    dma = pltpu.SemaphoreType.DMA
    gate_grad, up_grad, route_grad, down_grad = pl.pallas_call(
        kernel,
        out_shape=(
            jax.ShapeDtypeStruct((256, 256), BF16),
            jax.ShapeDtypeStruct((256, 256), BF16),
            jax.ShapeDtypeStruct((1, 256), F32),
            jax.ShapeDtypeStruct((20, 256), F32),
        ),
        in_specs=[vmem, vmem, vmem, vmem, pl.BlockSpec(memory_space=pltpu.SMEM), vmem],
        out_specs=(vmem, vmem, vmem, vmem),
        scratch_shapes=[
            pltpu.VMEM((40, 256), F32),
            pltpu.VMEM((24, 128), F32),
            pltpu.VMEM((40, 128), F32),
            pltpu.VMEM((4, 48, 128), BF16),
            pltpu.VMEM((8, 160, 128), BF16),
            pltpu.VMEM((2, 3, 4, 320, 128), BF16),
            pltpu.VMEM((12, 320, 128), F32),
            pltpu.VMEM((12, 320, 128), BF16),
            pltpu.VMEM((12, 320, 128), BF16),
            pltpu.VMEM((2, 4, 320, 128), BF16),
            pltpu.VMEM((2, 4, 320, 128), BF16),
            pltpu.VMEM((8, 160, 128), F32),
            pltpu.VMEM((8, 160, 128), BF16),
            pltpu.VMEM((7, 160, 128), BF16),
            pltpu.VMEM((4, 40, 128), F32),
            pltpu.VMEM((3, 40, 128), F32),
            pltpu.VMEM((24, 128), F32),
            pltpu.VMEM((24, 128), F32),
            pltpu.VMEM((8, 256), F32),
            pltpu.VMEM((3, 8, 256), F32),
            pltpu.VMEM((256, 256), BF16),
            pltpu.VMEM((256, 256), F32),
            pltpu.VMEM((256, 256), F32),
            dma((2,)), dma((2,)), dma((3,)), dma((3,)), dma((7,)), dma((7,)), dma((2,)), dma((2,)), dma((3,)), dma((3,)),
            dma((6,)), dma((6,)), dma((2, 4)), dma((2, 4)), dma((7,)), dma((7,)), dma((3,)), dma((3,)), dma((3,)), dma((3,)),
        ],
        compiler_params=pltpu.CompilerParams(
            collective_id=0, has_side_effects=True, vmem_limit_bytes=48 * 1024 * 1024
        ),
        cost_estimate=pl.CostEstimate(flops=1_006_632_960, bytes_accessed=3_000_000, transcendentals=65536),
    )(gate_pre, up_pre, out_grad, route_weight.reshape(1, 256), counts, down_weight)
    return (gate_grad, up_grad, route_grad.reshape(256), down_grad)


def solution(mesh):
    return jax.shard_map(
        on_device,
        mesh=mesh,
        in_specs=(
            P("dp", "expert"),
            P("dp", "expert"),
            P("dp", None),
            P("dp"),
            P("dp"),
            P("dp", "expert"),
        ),
        out_specs=(P("dp", "expert"), P("dp", "expert"), P("dp"), P("dp", "expert")),
        check_vma=False,
    )
```

time: 490 us -> 60.4 us (0.12)
  waiting for transfers between devices: 447 us -> 0 us
  Pallas kernels: 0 us -> 51.6 us
  between operations: 15.4 us -> 1.3 us
  blocking collectives: 8.38 us -> 0 us
  matrix products: 6.72 us -> 0 us
    unnamed x3 -> x0, waiting for transfers between devices: 316 us -> none
    all_gather x1 -> x0, waiting for transfers between devices: 131 us -> none  [on_device(): gathered = lax.all_gather(down_weight, 'dp', axis=0, tiled=True)]
    pallas_call x0 -> x1, Pallas kernels: none -> 51.6 us  [on_device(): pl.pallas_call(kernel, out_shape=(jax.ShapeDtypeStruct((256, 256), BF16),...]
    psum x1 -> x0, blocking collectives: 8.38 us -> none  [on_device(): route_grad = lax.psum(partial_match, 'expert') * live_mask]
    dot_general x3 -> x0, matrix products: 6.72 us -> none  [the longest x2 4.23 us: on_device(): lax.dot_general(scaled, hidden_half, (((0,), (0,)), ((), ())), preferred_...]
  transfers between devices with their start and end apart: 2 -> 0, of which waited for: 2 -> 0; matrix products, arithmetic and copies ran while one was open for 1% -> 0% of each run, Pallas kernels for 0% -> 0%
where the time goes in v1:
time: 60.4 us; the launch traced here: 60.2 us
  Pallas kernels  51.6 us (85%)
  local copies, waits for them, and re-layouts  7.21 us (12%)
  between operations  1.3 us (2%)
    pallas_call x1, Pallas kernels, on_device(): pl.pallas_call(kernel, out_shape=(jax.ShapeDtypeStruct((256, 256), BF16),...  51.6 us
    unnamed x14, local copies, waits for them, and re-layouts  7.21 us

profile of v1, /device:TPU:1, one launch (start us, length us, event | category | flops | bytes accessed | tf_op | source)
XLA Modules:
  0.0 60.2 jit_solution(9810958402028180521)
XLA Ops:
  1.3 0.0 copy-start
  1.3 1.5 %copy-done = bf16[256,3840]{1,0:T(8,128)(2,1)S(1)} copy-done((bf16[256,3840]{1,0:T(8,128)(2,1)S(1)}, bf16[256,3840]{1,0:T(8,128)(2,1)}, u32[]{:S(2)}) %copy-start) | copy-done | bytes 1966104
  2.8 0.0 copy-start.1
  2.8 0.9 %copy-done.1 = bf16[256,256]{1,0:T(8,128)(2,1)S(1)} copy-done((bf16[256,256]{1,0:T(8,128)(2,1)S(1)}, bf16[256,256]{1,0:T(8,128)(2,1)}, u32[]{:S(2)}) %copy-start.1) | copy-done | bytes 131096
  3.7 0.0 copy-start.2
  3.7 0.9 %copy-done.2 = bf16[256,256]{1,0:T(8,128)(2,1)S(1)} copy-done((bf16[256,256]{1,0:T(8,128)(2,1)S(1)}, bf16[256,256]{1,0:T(8,128)(2,1)}, u32[]{:S(2)}) %copy-start.2) | copy-done | bytes 131096
  4.6 0.0 copy-start.3
  4.6 0.7 %copy-done.3 = bf16[20,256]{1,0:T(8,128)(2,1)S(1)} copy-done((bf16[20,256]{1,0:T(8,128)(2,1)S(1)}, bf16[20,256]{1,0:T(8,128)(2,1)}, u32[]{:S(2)}) %copy-start.3) | copy-done | bytes 10264
  5.3 0.0 copy-start.4
  5.3 0.7 %copy-done.4 = f32[256]{0:T(256)S(1)} copy-done((f32[256]{0:T(256)S(1)}, f32[256]{0:T(256)}, u32[]{:S(2)}) %copy-start.4) | copy-done | bytes 1048
  6.0 51.6 %shard_map.93 = (bf16[256,256]{1,0:T(8,128)(2,1)S(1)}, bf16[256,256]{1,0:T(8,128)(2,1)S(1)}, f32[1,256]{1,0:T(1,128)S(1)}, f32[20,256]{1,0:T(8,128)S(1)}) custom-call(bf16[256,256]{1,0:T(8,128)(2,1)S(1)} %copy-done.1, bf16[256,256]{1,0:T(8,128)(2,1)S(1)} %copy-done.2, bf16[256,3840]{1,0:T(8,128)(2,1)S(1)} %copy-done, f32[1,256]{1,0:T(1,128)S(1)} %bitcast.3, ...), custom_call_target="tpu_custom_call" | custom-call | flops 1006632960 | bytes 3000000 | tf_op jit(solution)/shard_map/pallas_call | solution.py:179
  57.7 0.7 %copy.15 = bf16[256,256]{1,0:T(8,128)(2,1)} copy(bf16[256,256]{1,0:T(8,128)(2,1)S(1)} %get-tuple-element.16) | data formatting | bytes 262144
  58.3 0.7 %copy.16 = bf16[256,256]{1,0:T(8,128)(2,1)} copy(bf16[256,256]{1,0:T(8,128)(2,1)S(1)} %get-tuple-element.17) | data formatting | bytes 262144
  59.0 0.6 copy.17
  59.6 0.6 %copy.18 = f32[20,256]{1,0:T(8,128)} copy(f32[20,256]{1,0:T(8,128)S(1)} %get-tuple-element.19) | data formatting | bytes 40960
Async XLA Ops:
  1.3 1.5 %copy-start = (bf16[256,3840]{1,0:T(8,128)(2,1)S(1)}, bf16[256,3840]{1,0:T(8,128)(2,1)}, u32[]{:S(2)}) copy-start(bf16[256,3840]{1,0:T(8,128)(2,1)} %og_ref.1) | copy-start | bytes 5898244
  2.8 0.9 %copy-start.1 = (bf16[256,256]{1,0:T(8,128)(2,1)S(1)}, bf16[256,256]{1,0:T(8,128)(2,1)}, u32[]{:S(2)}) copy-start(bf16[256,256]{1,0:T(8,128)(2,1)} %gate_ref.1) | copy-start | bytes 393220
  3.7 0.9 %copy-start.2 = (bf16[256,256]{1,0:T(8,128)(2,1)S(1)}, bf16[256,256]{1,0:T(8,128)(2,1)}, u32[]{:S(2)}) copy-start(bf16[256,256]{1,0:T(8,128)(2,1)} %up_ref.1) | copy-start | bytes 393220
  4.6 0.7 %copy-start.3 = (bf16[20,256]{1,0:T(8,128)(2,1)S(1)}, bf16[20,256]{1,0:T(8,128)(2,1)}, u32[]{:S(2)}) copy-start(bf16[20,256]{1,0:T(8,128)(2,1)} %w_ref.1) | copy-start | bytes 30724
  5.3 0.7 %copy-start.4 = (f32[256]{0:T(256)S(1)}, f32[256]{0:T(256)}, u32[]{:S(2)}) copy-start(f32[256]{0:T(256)} %param.9) | copy-start | bytes 3076

commit v2 on v1

v2 whole, which is shorter than its diff:
```python
import math

import jax
import jax.numpy as jnp
from jax import lax
from jax.experimental import pallas as pl
from jax.experimental.pallas import tpu as pltpu
from jax.sharding import PartitionSpec as P

MESH = pl.DeviceIdType.MESH
F32, BF16 = jnp.float32, jnp.bfloat16


NEAR_FIRST = (0, 1, 7, 2, 6, 3, 5, 4)
FAR_FIRST = (4, 3, 5, 2, 6, 1, 7, 0)


def kernel(
    gate_hbm, up_hbm, og_hbm, weight_hbm, counts_hbm, w_hbm,
    gate_hbm_out, up_hbm_out, route_hbm_out, down_hbm_out,
    gate_out, up_out, route_out, down_out,
    gate_ref, up_ref, og_ref, weight_ref, counts_ref, w_ref,
    wf, g0_send, g0_recv, yb, wt, p_own, p_other, p_send, p_recv, r1_send, r1_recv,
    t_own, r2_send, r2_recv, u_own, r3_recv, f_send, f_recv, x_send, x_recv,
    hid, gate_co, up_co,
    in_s, out_s, pair_s, pair_r, far_s, far_r, y_s, y_r, near_s, near_r, fwd_s, fwd_r,
    psum_s, psum_r, r1_s, r1_r, r2_s, r2_r, r3_s, r3_r, x_s, x_r,
):
    me, x = lax.axis_index("dp"), lax.axis_index("expert")
    z, y, c = me // 16, lax.rem(me // 2, 8), lax.rem(me, 2)
    zdiv, zmod = z // 3, lax.rem(z, 3)
    first = c == 0

    def at(dz=0, dy=0, dc=0):
        return {"dp": lax.rem(z + dz, 12) * 16 + lax.rem(y + dy, 8) * 2 + lax.rem(c + dc, 2)}

    def across(k):
        return {"expert": lax.rem(x + k, 4)}

    def send(src, dst, ssem, rsem, device):
        copy = pltpu.make_async_remote_copy(
            src_ref=src, dst_ref=dst, send_sem=ssem, recv_sem=rsem, device_id=device, device_id_type=MESH
        )
        copy.start()
        return copy

    incoming = []
    for k, (src, dst) in enumerate((
        (w_hbm, w_ref), (counts_hbm, counts_ref), (weight_hbm, weight_ref),
        (gate_hbm, gate_ref), (up_hbm, up_ref), (og_hbm, og_ref),
    )):
        incoming.append(pltpu.make_async_copy(src, dst, in_s.at[k]))
        incoming[-1].start()
    barrier = pltpu.get_barrier_semaphore()
    partners = [at(dz=d) for d in (6, 3, 9)] + [at(dy=d) for d in (4, 3, 5, 2, 6, 1, 7)]
    partners += [at(dz=1), at(dz=11), at(dc=1)] + [across(k) for k in (2, 1, 3)]
    for device in partners:
        pl.semaphore_signal(barrier, inc=1, device_id=device, device_id_type=MESH)

    wf[...] = jnp.zeros_like(wf)
    g0_recv[24:40, :] = jnp.zeros((16, 128), F32)
    incoming[0].wait()
    wf[0:20, :] = w_ref[...].astype(F32)
    g0_send[...] = jnp.where(first, wf[0:24, 128:256], wf[0:24, 0:128])

    for k in range(1, 5):
        incoming[k].wait()
    eye = lax.broadcasted_iota(jnp.int32, (256, 256), 0) == lax.broadcasted_iota(jnp.int32, (256, 256), 1)
    live_row = (lax.broadcasted_iota(jnp.int32, (1, 256), 1) < counts_ref[...]).astype(F32)
    scale_row = weight_ref[...] * live_row
    scale = jnp.sum(jnp.where(eye, jnp.broadcast_to(scale_row, (256, 256)), 0.0), axis=1, keepdims=True)
    gate, up = gate_ref[...].astype(F32), up_ref[...].astype(F32)
    sig = jax.nn.sigmoid(gate)
    act = gate * sig
    hid[...] = (act * up).astype(BF16)
    gate_co[...] = scale * up * sig * (1.0 + gate * (1.0 - sig))
    up_co[...] = scale * act
    incoming[5].wait()

    def shares(ks):
        for k in ks:
            scaled = (og_ref[:, 640 * k : 640 * (k + 1)].astype(F32) * scale).astype(BF16)
            part = lax.dot_general(scaled, hid[...], (((0,), (0,)), ((), ())), preferred_element_type=F32)
            lo, hi = part[:, 0:128], part[:, 128:256]
            own, other = jnp.where(first, lo, hi), jnp.where(first, hi, lo)
            for b in (0, 1):
                m, j = (2 * k + b) % 3, (2 * k + b) // 3
                for i in range(8):
                    at_row = 320 * b + 40 * i
                    p_own[m, i, 40 * j : 40 * j + 40, :] = own[at_row : at_row + 40]
                    p_other[m, i, 40 * j : 40 * j + 40, :] = other[at_row : at_row + 40]

    shares(range(6))
    pl.semaphore_wait(barrier, len(partners))
    pair = send(g0_send, g0_recv.at[pl.ds(0, 24)], pair_s.at[0], pair_r.at[0], at(dc=1))
    pair.wait_recv()
    mine = jnp.where(first, wf[:, 0:128], wf[:, 128:256])
    other = g0_recv[...]
    block = jnp.where(first, mine + pltpu.roll(other, 20, 0), other + pltpu.roll(mine, 20, 0))
    yb[y, zdiv] = jnp.concatenate([block, jnp.zeros((8, 128), F32)], axis=0).astype(BF16)
    piece = yb.at[y, zdiv]
    fars = {k: send(piece, piece, far_s.at[k - 1], far_r.at[k - 1], at(dz=3 * k)) for k in (2, 1, 3)}
    ys = {}

    def along_y(k):
        piece = yb.at[y, lax.rem(zdiv + 4 - k, 4)]
        for d in NEAR_FIRST[1:]:
            ys[k, d] = send(piece, piece, y_s.at[k, d], y_r.at[k, d], at(dy=d))

    along_y(0)

    psums = []
    for k in (1, 2, 0):
        m = lax.rem(zmod + k, 3)
        p_send[m] = p_other[m].astype(BF16)
        psums.append(send(p_send.at[m], p_recv.at[m], psum_s.at[k], psum_r.at[k], at(dc=1)))

    r1s = {}
    psums[0].wait_recv()
    psums[1].wait_recv()
    for d in FAR_FIRST:
        i = lax.rem(y + d, 8)
        for side, step in enumerate((1, 11)):
            m = lax.rem(zmod + step, 3)
            r1_send[side, i] = (p_own[m, i] + p_recv[m, i].astype(F32)).astype(BF16)
            r1s[side, d] = send(
                r1_send.at[side, i], r1_recv.at[side, i], r1_s.at[side, d], r1_r.at[side, d], at(dz=step)
            )

    for k in (1, 3, 2):
        fars[k].wait_recv()
        along_y(k)
    nears, fwds = {}, []

    def forward(m, i, sem):
        piece = wt.at[c, m, i]
        fwds.append(send(piece, piece, fwd_s.at[sem], fwd_r.at[sem], at(dc=1)))

    psums[2].wait_recv()
    r2s = {}
    for n in range(8):
        d = NEAR_FIRST[n]
        if d:
            for k in range(4):
                ys[k, d].wait_recv()
        i = lax.rem(y + 8 - d, 8)
        wt[c, zmod, i] = jnp.concatenate([yb[i, j].astype(F32)[0:40] for j in range(4)], axis=0).astype(BF16)
        for side, step in enumerate((1, 11)):
            piece = wt.at[c, zmod, i]
            nears[side, d] = send(piece, piece, near_s.at[side, d], near_r.at[side, d], at(dz=step))
        forward(zmod, i, d)
        d = FAR_FIRST[n]
        r1s[0, d].wait_recv()
        r1s[1, d].wait_recv()
        i = lax.rem(y + d, 8)
        total = p_own[zmod, i] + p_recv[zmod, i].astype(F32)
        total = total + (r1_recv[0, i].astype(F32) + r1_recv[1, i].astype(F32))
        if d:
            r2_send[d - 1] = total.astype(BF16)
            r2s[d] = send(r2_send.at[d - 1], r2_recv.at[d - 1], r2_s.at[d - 1], r2_r.at[d - 1], at(dy=d))
        else:
            t_own[...] = total

    for n in range(8):
        d = NEAR_FIRST[n]
        i = lax.rem(y + 8 - d, 8)
        for side in range(2):
            nears[side, d].wait_recv()
            forward(lax.rem(zmod + 2 - side, 3), i, 8 * side + 8 + d)

    total = t_own[...]
    for d in NEAR_FIRST[1:]:
        r2s[d].wait_recv()
        total = total + r2_recv[d - 1].astype(F32)
    u_own[...] = total.reshape(4, 40, 128)
    r3s = [
        send(u_own.at[lax.rem(zdiv + k, 4)], r3_recv.at[k - 1], r3_s.at[k - 1], r3_r.at[k - 1], at(dz=3 * k))
        for k in (2, 1, 3)
    ]

    for copy in fwds:
        copy.wait_recv()
    proj = None
    for k in range(6):
        halves = []
        for h in range(2):
            rows = [
                wt[h, b % 3, i].astype(F32)[40 * (b // 3) : 40 * (b // 3) + 40] for b in (2 * k, 2 * k + 1) for i in range(8)
            ]
            halves.append(jnp.concatenate(rows, axis=0).astype(BF16))
        term = jnp.dot(
            og_ref[:, 640 * k : 640 * (k + 1)], jnp.concatenate(halves, axis=1), preferred_element_type=F32
        )
        proj = term if proj is None else proj + term
    match = jnp.sum(hid[...].astype(F32) * proj, axis=1, keepdims=True)
    match_row = jnp.sum(jnp.where(eye, jnp.broadcast_to(match, (256, 256)), 0.0), axis=0, keepdims=True)
    x_send[...] = jnp.broadcast_to(match_row, (8, 256))
    xs = [send(x_send, x_recv.at[k - 1], x_s.at[k - 1], x_r.at[k - 1], across(k)) for k in (2, 1, 3)]
    gate_out[...] = (proj * gate_co[...]).astype(BF16)
    up_out[...] = (proj * up_co[...]).astype(BF16)
    outgoing = [pltpu.make_async_copy(gate_out, gate_hbm_out, out_s.at[0]), pltpu.make_async_copy(up_out, up_hbm_out, out_s.at[1])]
    for copy in outgoing:
        copy.start()

    for copy in r3s:
        copy.wait_recv()
    total = (u_own[zdiv] + r3_recv[0] + (r3_recv[1] + r3_recv[2])) * (1.0 / math.sqrt(49152))
    turned = pltpu.roll(total, 20, 0)
    f_send[...] = jnp.where(first, turned, total)[0:24]
    final = send(f_send, f_recv, pair_s.at[1], pair_r.at[1], at(dc=1))
    keep = jnp.where(first, total, turned)[0:24]
    final.wait_recv()
    got = f_recv[...]
    down_out[:, 0:128] = jnp.where(first, keep, got)[0:20]
    down_out[:, 128:256] = jnp.where(first, got, keep)[0:20]
    outgoing.append(pltpu.make_async_copy(down_out, down_hbm_out, out_s.at[2]))
    outgoing[-1].start()

    for copy in xs:
        copy.wait_recv()
    everyone = x_send[...] + x_recv[0] + (x_recv[1] + x_recv[2])
    route_out[...] = everyone[0:1] * live_row
    outgoing.append(pltpu.make_async_copy(route_out, route_hbm_out, out_s.at[3]))
    outgoing[-1].start()
    waiting = [pair, final] + fwds + psums + r3s + xs
    for group in (fars, ys, nears, r1s, r2s):
        waiting += [group[key] for key in group]
    for copy in waiting:
        copy.wait_send()
    for copy in outgoing:
        copy.wait()


def hand_over(a_in, b_in, c_in, d_in, a_out, b_out, c_out, d_out, a_mid, b_mid, c_mid, d_mid, sem_in, sem_out):
    first = [
        pltpu.make_async_copy(src, dst, sem_in.at[k])
        for k, (src, dst) in enumerate(((a_in, a_mid), (b_in, b_mid), (c_in, c_mid), (d_in, d_mid)))
    ]
    second = [
        pltpu.make_async_copy(src, dst, sem_out.at[k])
        for k, (src, dst) in enumerate(((a_mid, a_out), (b_mid, b_out), (c_mid, c_out), (d_mid, d_out)))
    ]
    for copy in first:
        copy.start()
    for k in range(4):
        first[k].wait()
        second[k].start()
    for copy in second:
        copy.wait()


def on_device(gate_pre, up_pre, out_grad, route_weight, counts, down_weight):
    hbm = pl.BlockSpec(memory_space=pl.ANY)
    dma = pltpu.SemaphoreType.DMA
    shapes = (
        jax.ShapeDtypeStruct((256, 256), BF16),
        jax.ShapeDtypeStruct((256, 256), BF16),
        jax.ShapeDtypeStruct((1, 256), F32),
        jax.ShapeDtypeStruct((20, 256), F32),
    )
    results = pl.pallas_call(
        kernel,
        out_shape=shapes,
        in_specs=[hbm] * 6,
        out_specs=(hbm, hbm, hbm, hbm),
        scratch_shapes=[
            pltpu.VMEM((256, 256), BF16),
            pltpu.VMEM((256, 256), BF16),
            pltpu.VMEM((1, 256), F32),
            pltpu.VMEM((20, 256), F32),
            pltpu.VMEM((256, 256), BF16),
            pltpu.VMEM((256, 256), BF16),
            pltpu.VMEM((256, 3840), BF16),
            pltpu.VMEM((1, 256), F32),
            pltpu.VMEM((1, 1), jnp.int32),
            pltpu.VMEM((20, 256), BF16),
            pltpu.VMEM((40, 256), F32),
            pltpu.VMEM((24, 128), F32),
            pltpu.VMEM((40, 128), F32),
            pltpu.VMEM((8, 4, 48, 128), BF16),
            pltpu.VMEM((2, 3, 8, 160, 128), BF16),
            pltpu.VMEM((3, 8, 160, 128), F32),
            pltpu.VMEM((3, 8, 160, 128), F32),
            pltpu.VMEM((3, 8, 160, 128), BF16),
            pltpu.VMEM((3, 8, 160, 128), BF16),
            pltpu.VMEM((2, 8, 160, 128), BF16),
            pltpu.VMEM((2, 8, 160, 128), BF16),
            pltpu.VMEM((160, 128), F32),
            pltpu.VMEM((7, 160, 128), BF16),
            pltpu.VMEM((7, 160, 128), BF16),
            pltpu.VMEM((4, 40, 128), F32),
            pltpu.VMEM((3, 40, 128), F32),
            pltpu.VMEM((24, 128), F32),
            pltpu.VMEM((24, 128), F32),
            pltpu.VMEM((8, 256), F32),
            pltpu.VMEM((3, 8, 256), F32),
            pltpu.VMEM((256, 256), BF16),
            pltpu.VMEM((256, 256), F32),
            pltpu.VMEM((256, 256), F32),
            dma((6,)), dma((4,)), dma((2,)), dma((2,)), dma((3,)), dma((3,)), dma((4, 8)), dma((4, 8)),
            dma((2, 8)), dma((2, 8)), dma((24,)), dma((24,)), dma((3,)), dma((3,)), dma((2, 8)), dma((2, 8)),
            dma((7,)), dma((7,)), dma((3,)), dma((3,)), dma((3,)), dma((3,)),
        ],
        compiler_params=pltpu.CompilerParams(
            collective_id=0, has_side_effects=True, vmem_limit_bytes=48 * 1024 * 1024
        ),
        cost_estimate=pl.CostEstimate(flops=1_006_632_960, bytes_accessed=3_000_000, transcendentals=65536),
    )(gate_pre, up_pre, out_grad, route_weight.reshape(1, 256), counts.reshape(1, 1), down_weight)
    gate_grad, up_grad, route_grad, down_grad = pl.pallas_call(
        hand_over,
        out_shape=shapes,
        in_specs=[hbm] * 4,
        out_specs=(hbm, hbm, hbm, hbm),
        scratch_shapes=[
            pltpu.VMEM((256, 256), BF16),
            pltpu.VMEM((256, 256), BF16),
            pltpu.VMEM((1, 256), F32),
            pltpu.VMEM((20, 256), F32),
            dma((4,)),
            dma((4,)),
        ],
        compiler_params=pltpu.CompilerParams(vmem_limit_bytes=48 * 1024 * 1024),
    )(*results)
    return (gate_grad, up_grad, route_grad.reshape(256), down_grad)


def solution(mesh):
    return jax.shard_map(
        on_device,
        mesh=mesh,
        in_specs=(
            P("dp", "expert"),
            P("dp", "expert"),
            P("dp", None),
            P("dp"),
            P("dp"),
            P("dp", "expert"),
        ),
        out_specs=(P("dp", "expert"), P("dp", "expert"), P("dp"), P("dp", "expert")),
        check_vma=False,
    )
```

time: 60.4 us -> 57.3 us (0.949)
  local copies, waits for them, and re-layouts: 7.21 us -> 4.73 us
    unnamed x14 -> x10, local copies, waits for them, and re-layouts: 7.21 us -> 4.73 us
    pallas_call x1 -> x2, Pallas kernels: 51.6 us -> 51 us  [the longest x1 49.9 us: on_device(): pl.pallas_call(kernel, out_shape=shapes, in_specs=[hbm] * 6, out_specs=(h...]
where the time goes in v2:
time: 57.3 us; the launch traced here: 57.1 us
  Pallas kernels  51 us (89%)
  local copies, waits for them, and re-layouts  4.73 us (8%)
  between operations  1.3 us (2%)
    pallas_call x1, Pallas kernels, on_device(): pl.pallas_call(kernel, out_shape=shapes, in_specs=[hbm] * 6, out_specs=(h...  49.9 us
    unnamed x10, local copies, waits for them, and re-layouts  4.73 us

profile of v2, /device:TPU:1, one launch (start us, length us, event | category | flops | bytes accessed | tf_op | source)
XLA Modules:
  0.0 57.1 jit_solution(11666743038418993724)
XLA Ops:
  1.3 0.0 copy-start
  1.3 1.5 %copy-done = bf16[256,3840]{1,0:T(8,128)(2,1)S(1)} copy-done((bf16[256,3840]{1,0:T(8,128)(2,1)S(1)}, bf16[256,3840]{1,0:T(8,128)(2,1)}, u32[]{:S(2)}) %copy-start) | copy-done | bytes 1966104
  2.8 0.0 copy-start.1
  2.8 0.9 %copy-done.1 = bf16[256,256]{1,0:T(8,128)(2,1)S(1)} copy-done((bf16[256,256]{1,0:T(8,128)(2,1)S(1)}, bf16[256,256]{1,0:T(8,128)(2,1)}, u32[]{:S(2)}) %copy-start.1) | copy-done | bytes 131096
  3.7 0.0 copy-start.2
  3.7 0.9 %copy-done.2 = bf16[256,256]{1,0:T(8,128)(2,1)S(1)} copy-done((bf16[256,256]{1,0:T(8,128)(2,1)S(1)}, bf16[256,256]{1,0:T(8,128)(2,1)}, u32[]{:S(2)}) %copy-start.2) | copy-done | bytes 131096
  4.6 0.0 copy-start.3
  4.6 0.7 %copy-done.3 = bf16[20,256]{1,0:T(8,128)(2,1)S(1)} copy-done((bf16[20,256]{1,0:T(8,128)(2,1)S(1)}, bf16[20,256]{1,0:T(8,128)(2,1)}, u32[]{:S(2)}) %copy-start.3) | copy-done | bytes 10264
  5.3 0.0 copy-start.4
  5.3 0.7 %copy-done.4 = f32[256]{0:T(256)S(1)} copy-done((f32[256]{0:T(256)S(1)}, f32[256]{0:T(256)}, u32[]{:S(2)}) %copy-start.4) | copy-done | bytes 1048
  6.0 49.9 %shard_map.93 = (bf16[256,256]{1,0:T(8,128)(2,1)S(1)}, bf16[256,256]{1,0:T(8,128)(2,1)S(1)}, f32[1,256]{1,0:T(1,128)S(1)}, f32[20,256]{1,0:T(8,128)S(1)}) custom-call(bf16[256,256]{1,0:T(8,128)(2,1)S(1)} %copy-done.1, bf16[256,256]{1,0:T(8,128)(2,1)S(1)} %copy-done.2, bf16[256,3840]{1,0:T(8,128)(2,1)S(1)} %copy-done, f32[1,256]{1,0:T(1,128)S(1)} %bitcast.4, ...), custom_call_target="tpu_custom_call" | custom-call | flops 1006632960 | bytes 3000000 | tf_op jit(solution)/shard_map/pallas_call | solution.py:261
  55.9 1.1 %shard_map.94 = (bf16[256,256]{1,0:T(8,128)(2,1)}, bf16[256,256]{1,0:T(8,128)(2,1)}, f32[1,256]{1,0:T(1,128)}, f32[20,256]{1,0:T(8,128)}) custom-call(bf16[256,256]{1,0:T(8,128)(2,1)S(1)} %get-tuple-element.12.a_in, bf16[256,256]{1,0:T(8,128)(2,1)S(1)} %get-tuple-element.13.b_in, f32[1,256]{1,0:T(1,128)S(1)} %get-tuple-element.14.c_in, ...), custom_call_target="tpu_custom_call" | custom-call | tf_op jit(solution)/shard_map/pallas_call | solution.py:309
Async XLA Ops:
  1.3 1.5 %copy-start = (bf16[256,3840]{1,0:T(8,128)(2,1)S(1)}, bf16[256,3840]{1,0:T(8,128)(2,1)}, u32[]{:S(2)}) copy-start(bf16[256,3840]{1,0:T(8,128)(2,1)} %og_hbm.1) | copy-start | bytes 5898244
  2.8 0.9 %copy-start.1 = (bf16[256,256]{1,0:T(8,128)(2,1)S(1)}, bf16[256,256]{1,0:T(8,128)(2,1)}, u32[]{:S(2)}) copy-start(bf16[256,256]{1,0:T(8,128)(2,1)} %gate_hbm.1) | copy-start | bytes 393220
  3.7 0.9 %copy-start.2 = (bf16[256,256]{1,0:T(8,128)(2,1)S(1)}, bf16[256,256]{1,0:T(8,128)(2,1)}, u32[]{:S(2)}) copy-start(bf16[256,256]{1,0:T(8,128)(2,1)} %up_hbm.1) | copy-start | bytes 393220
  4.6 0.7 %copy-start.3 = (bf16[20,256]{1,0:T(8,128)(2,1)S(1)}, bf16[20,256]{1,0:T(8,128)(2,1)}, u32[]{:S(2)}) copy-start(bf16[20,256]{1,0:T(8,128)(2,1)} %w_hbm.1) | copy-start | bytes 30724
  5.3 0.7 %copy-start.4 = (f32[256]{0:T(256)S(1)}, f32[256]{0:T(256)}, u32[]{:S(2)}) copy-start(f32[256]{0:T(256)} %param.9) | copy-start | bytes 3076

commit v3 on v2

--- a/solution.py
+++ b/solution.py
@@ -302,7 +302,7 @@
             dma((7,)), dma((7,)), dma((3,)), dma((3,)), dma((3,)), dma((3,)),
         ],
         compiler_params=pltpu.CompilerParams(
-            collective_id=0, has_side_effects=True, vmem_limit_bytes=48 * 1024 * 1024
+            collective_id=0, has_side_effects=True, vmem_limit_bytes=56 * 1024 * 1024
         ),
         cost_estimate=pl.CostEstimate(flops=1_006_632_960, bytes_accessed=3_000_000, transcendentals=65536),
     )(gate_pre, up_pre, out_grad, route_weight.reshape(1, 256), counts.reshape(1, 1), down_weight)
@@ -319,7 +319,7 @@
             dma((4,)),
             dma((4,)),
         ],
-        compiler_params=pltpu.CompilerParams(vmem_limit_bytes=48 * 1024 * 1024),
+        compiler_params=pltpu.CompilerParams(vmem_limit_bytes=56 * 1024 * 1024),
     )(*results)
     return (gate_grad, up_grad, route_grad.reshape(256), down_grad)
 

time: 57.3 us -> 53.6 us (0.935)
  local copies, waits for them, and re-layouts: 4.73 us -> 0 us
  Pallas kernels: 51 us -> 52.1 us
    unnamed x10 -> x0, local copies, waits for them, and re-layouts: 4.73 us -> none
where the time goes in v3:
time: 53.6 us; the launch traced here: 53.4 us
  Pallas kernels  52.1 us (97%)
  between operations  1.29 us (2%)
    pallas_call x1, Pallas kernels, on_device(): pl.pallas_call(kernel, out_shape=shapes, in_specs=[hbm] * 6, out_specs=(h...  50.4 us
    pallas_call x1, Pallas kernels, on_device(): pl.pallas_call(hand_over, out_shape=shapes, in_specs=[hbm] * 4, out_specs...  1.7 us

profile of v3, /device:TPU:1, one launch (start us, length us, event | category | flops | bytes accessed | tf_op | source)
XLA Modules:
  0.0 53.4 jit_solution(4780535373649605621)
XLA Ops:
  1.3 50.4 %shard_map.93 = (bf16[256,256]{1,0:T(8,128)(2,1)}, bf16[256,256]{1,0:T(8,128)(2,1)}, f32[1,256]{1,0:T(1,128)}, f32[20,256]{1,0:T(8,128)}) custom-call(bf16[256,256]{1,0:T(8,128)(2,1)} %gate_hbm.1, bf16[256,256]{1,0:T(8,128)(2,1)} %up_hbm.1, bf16[256,3840]{1,0:T(8,128)(2,1)} %og_hbm.1, f32[1,256]{1,0:T(1,128)} %bitcast.4, s32[1,1]{1,0:T(1,128)} %bitcast.3.counts_hbm, ...), custom_call_target="tpu_custom_call" | custom-call | flops 1006632960 | bytes 3000000 | tf_op jit(solution)/shard_map/pallas_call | solution.py:261
  51.7 1.7 %shard_map.94 = (bf16[256,256]{1,0:T(8,128)(2,1)}, bf16[256,256]{1,0:T(8,128)(2,1)}, f32[1,256]{1,0:T(1,128)}, f32[20,256]{1,0:T(8,128)}) custom-call(bf16[256,256]{1,0:T(8,128)(2,1)} %get-tuple-element.12.a_in, bf16[256,256]{1,0:T(8,128)(2,1)} %get-tuple-element.13.b_in, f32[1,256]{1,0:T(1,128)} %get-tuple-element.14.c_in, f32[20,256]{1,0:T(8,128)} %get-tuple-element.15.d_in), custom_call_target="tpu_custom_call" | custom-call | tf_op jit(solution)/shard_map/pallas_call | solution.py:309

commit v4 on v3

--- a/solution.py
+++ b/solution.py
@@ -12,7 +12,8 @@
 
 
 NEAR_FIRST = (0, 1, 7, 2, 6, 3, 5, 4)
-FAR_FIRST = (4, 3, 5, 2, 6, 1, 7, 0)
+SUM_ORDER = (2, 6, 4, 3, 5, 1, 7, 0)
+GROUPS = ((0, 3), (3, 2), (5, 3))
 
 
 def kernel(
@@ -22,7 +23,7 @@
     gate_ref, up_ref, og_ref, weight_ref, counts_ref, w_ref,
     wf, g0_send, g0_recv, yb, wt, p_own, p_other, p_send, p_recv, r1_send, r1_recv,
     t_own, r2_send, r2_recv, u_own, r3_recv, f_send, f_recv, x_send, x_recv,
-    hid, gate_co, up_co,
+    hid, gate_co, up_co, wn,
     in_s, out_s, pair_s, pair_r, far_s, far_r, y_s, y_r, near_s, near_r, fwd_s, fwd_r,
     psum_s, psum_r, r1_s, r1_r, r2_s, r2_r, r3_s, r3_r, x_s, x_r,
 ):
@@ -91,82 +92,108 @@
                     p_other[m, i, 40 * j : 40 * j + 40, :] = other[at_row : at_row + 40]
 
     shares(range(6))
+    for m in range(3):
+        p_send[m] = p_other[m].astype(BF16)
     pl.semaphore_wait(barrier, len(partners))
     pair = send(g0_send, g0_recv.at[pl.ds(0, 24)], pair_s.at[0], pair_r.at[0], at(dc=1))
+    psums = []
+    for k in (1, 2, 0):
+        m = lax.rem(zmod + k, 3)
+        psums.append(send(p_send.at[m], p_recv.at[m], psum_s.at[k], psum_r.at[k], at(dc=1)))
+
     pair.wait_recv()
     mine = jnp.where(first, wf[:, 0:128], wf[:, 128:256])
     other = g0_recv[...]
     block = jnp.where(first, mine + pltpu.roll(other, 20, 0), other + pltpu.roll(mine, 20, 0))
-    yb[y, zdiv] = jnp.concatenate([block, jnp.zeros((8, 128), F32)], axis=0).astype(BF16)
-    piece = yb.at[y, zdiv]
-    fars = {k: send(piece, piece, far_s.at[k - 1], far_r.at[k - 1], at(dz=3 * k)) for k in (2, 1, 3)}
+    def z_slot(k):
+        return k + (k // 2) * (1 - 2 * (k // 3))
+
+    def y_slot(d):
+        return (1 - d // 5) * (2 * d - 1) + (d // 5) * (16 - 2 * d) + (7 - d) // 7
+
+    yb[0, 0] = jnp.concatenate([block, jnp.zeros((8, 128), F32)], axis=0).astype(BF16)
+    fars = {
+        k: send(yb.at[0, 0], yb.at[0, z_slot(k)], far_s.at[k - 1], far_r.at[k - 1], at(dz=3 * k)) for k in (2, 1, 3)
+    }
     ys = {}
 
-    def along_y(k):
-        piece = yb.at[y, lax.rem(zdiv + 4 - k, 4)]
+    def along_y(part, slots):
         for d in NEAR_FIRST[1:]:
-            ys[k, d] = send(piece, piece, y_s.at[k, d], y_r.at[k, d], at(dy=d))
-
-    along_y(0)
-
-    psums = []
-    for k in (1, 2, 0):
-        m = lax.rem(zmod + k, 3)
-        p_send[m] = p_other[m].astype(BF16)
-        psums.append(send(p_send.at[m], p_recv.at[m], psum_s.at[k], psum_r.at[k], at(dc=1)))
+            ys[part, d] = send(
+                yb.at[0, slots], yb.at[y_slot(d), slots], y_s.at[part, d], y_r.at[part, d], at(dy=d)
+            )
+
+    along_y(0, pl.ds(0, 1))
 
     r1s = {}
     psums[0].wait_recv()
     psums[1].wait_recv()
-    for d in FAR_FIRST:
-        i = lax.rem(y + d, 8)
+    for g, (start, size) in enumerate(GROUPS):
         for side, step in enumerate((1, 11)):
             m = lax.rem(zmod + step, 3)
-            r1_send[side, i] = (p_own[m, i] + p_recv[m, i].astype(F32)).astype(BF16)
-            r1s[side, d] = send(
-                r1_send.at[side, i], r1_recv.at[side, i], r1_s.at[side, d], r1_r.at[side, d], at(dz=step)
+            for n in range(start, start + size):
+                i = lax.rem(y + SUM_ORDER[n], 8)
+                r1_send[side, n] = (p_own[m, i] + p_recv[m, i].astype(F32)).astype(BF16)
+            span = pl.ds(start, size)
+            r1s[side, g] = send(
+                r1_send.at[side, span], r1_recv.at[side, span], r1_s.at[side, g], r1_r.at[side, g], at(dz=step)
             )
 
-    for k in (1, 3, 2):
-        fars[k].wait_recv()
-        along_y(k)
+    fars[1].wait_recv()
+    fars[3].wait_recv()
+    along_y(1, pl.ds(1, 2))
+    fars[2].wait_recv()
+    along_y(2, pl.ds(3, 1))
     nears, fwds = {}, []
 
-    def forward(m, i, sem):
-        piece = wt.at[c, m, i]
+    def forward(m, g, sem):
+        piece = wt.at[c, m, pl.ds(GROUPS[g][0], GROUPS[g][1])]
         fwds.append(send(piece, piece, fwd_s.at[sem], fwd_r.at[sem], at(dc=1)))
 
     psums[2].wait_recv()
     r2s = {}
-    for n in range(8):
-        d = NEAR_FIRST[n]
-        if d:
-            for k in range(4):
-                ys[k, d].wait_recv()
-        i = lax.rem(y + 8 - d, 8)
-        wt[c, zmod, i] = jnp.concatenate([yb[i, j].astype(F32)[0:40] for j in range(4)], axis=0).astype(BF16)
+    z_slots = [z_slot(lax.rem(zdiv + 4 - j, 4)) for j in range(4)]
+    for g, (start, size) in enumerate(GROUPS):
+        for n in range(start, start + size):
+            d = NEAR_FIRST[n]
+            if d:
+                for part in range(3):
+                    ys[part, d].wait_recv()
+            rows = [yb[n, z_slots[j]].astype(F32)[0:40] for j in range(4)]
+            wt[c, zmod, n] = jnp.concatenate(rows, axis=0).astype(BF16)
+        piece = wt.at[c, zmod, pl.ds(start, size)]
         for side, step in enumerate((1, 11)):
-            piece = wt.at[c, zmod, i]
-            nears[side, d] = send(piece, piece, near_s.at[side, d], near_r.at[side, d], at(dz=step))
-        forward(zmod, i, d)
-        d = FAR_FIRST[n]
-        r1s[0, d].wait_recv()
-        r1s[1, d].wait_recv()
-        i = lax.rem(y + d, 8)
-        total = p_own[zmod, i] + p_recv[zmod, i].astype(F32)
-        total = total + (r1_recv[0, i].astype(F32) + r1_recv[1, i].astype(F32))
-        if d:
-            r2_send[d - 1] = total.astype(BF16)
-            r2s[d] = send(r2_send.at[d - 1], r2_recv.at[d - 1], r2_s.at[d - 1], r2_r.at[d - 1], at(dy=d))
-        else:
-            t_own[...] = total
-
-    for n in range(8):
-        d = NEAR_FIRST[n]
-        i = lax.rem(y + 8 - d, 8)
+            nears[side, g] = send(piece, piece, near_s.at[side, g], near_r.at[side, g], at(dz=step))
+        forward(zmod, g, g)
+        r1s[0, g].wait_recv()
+        r1s[1, g].wait_recv()
+        for n in range(start, start + size):
+            d = SUM_ORDER[n]
+            i = lax.rem(y + d, 8)
+            total = p_own[zmod, i] + p_recv[zmod, i].astype(F32)
+            total = total + (r1_recv[0, n].astype(F32) + r1_recv[1, n].astype(F32))
+            if d:
+                r2_send[d - 1] = total.astype(BF16)
+                r2s[d] = send(r2_send.at[d - 1], r2_recv.at[d - 1], r2_s.at[d - 1], r2_r.at[d - 1], at(dy=d))
+            else:
+                t_own[...] = total
+
+    def settle(h, m):
+        for j in range(4):
+            rows = [wt[h, m, y_slots[i]].astype(F32)[40 * j : 40 * j + 40] for i in range(8)]
+            wn[h, 3 * j + m] = jnp.concatenate(rows, axis=0).astype(BF16)
+
+    y_slots = [y_slot(lax.rem(y + 8 - i, 8)) for i in range(8)]
+    settle(c, zmod)
+    for copy in fwds[:3]:
+        copy.wait_recv()
+    settle(1 - c, zmod)
+    for g in range(3):
         for side in range(2):
-            nears[side, d].wait_recv()
-            forward(lax.rem(zmod + 2 - side, 3), i, 8 * side + 8 + d)
+            nears[side, g].wait_recv()
+            forward(lax.rem(zmod + 2 - side, 3), g, 3 * side + 3 + g)
+    for side in range(2):
+        settle(c, lax.rem(zmod + 2 - side, 3))
 
     total = t_own[...]
     for d in NEAR_FIRST[1:]:
@@ -178,19 +205,14 @@
         for k in (2, 1, 3)
     ]
 
-    for copy in fwds:
+    for copy in fwds[3:]:
         copy.wait_recv()
+    for side in range(2):
+        settle(1 - c, lax.rem(zmod + 2 - side, 3))
     proj = None
     for k in range(6):
-        halves = []
-        for h in range(2):
-            rows = [
-                wt[h, b % 3, i].astype(F32)[40 * (b // 3) : 40 * (b // 3) + 40] for b in (2 * k, 2 * k + 1) for i in range(8)
-            ]
-            halves.append(jnp.concatenate(rows, axis=0).astype(BF16))
-        term = jnp.dot(
-            og_ref[:, 640 * k : 640 * (k + 1)], jnp.concatenate(halves, axis=1), preferred_element_type=F32
-        )
+        both = jnp.concatenate([wn[h, 2 * k : 2 * k + 2].reshape(640, 128) for h in range(2)], axis=1)
+        term = jnp.dot(og_ref[:, 640 * k : 640 * (k + 1)], both, preferred_element_type=F32)
         proj = term if proj is None else proj + term
     match = jnp.sum(hid[...].astype(F32) * proj, axis=1, keepdims=True)
     match_row = jnp.sum(jnp.where(eye, jnp.broadcast_to(match, (256, 256)), 0.0), axis=0, keepdims=True)
@@ -297,8 +319,9 @@
             pltpu.VMEM((256, 256), BF16),
             pltpu.VMEM((256, 256), F32),
             pltpu.VMEM((256, 256), F32),
-            dma((6,)), dma((4,)), dma((2,)), dma((2,)), dma((3,)), dma((3,)), dma((4, 8)), dma((4, 8)),
-            dma((2, 8)), dma((2, 8)), dma((24,)), dma((24,)), dma((3,)), dma((3,)), dma((2, 8)), dma((2, 8)),
+            pltpu.VMEM((2, 12, 320, 128), BF16),
+            dma((6,)), dma((4,)), dma((2,)), dma((2,)), dma((3,)), dma((3,)), dma((3, 8)), dma((3, 8)),
+            dma((2, 3)), dma((2, 3)), dma((9,)), dma((9,)), dma((3,)), dma((3,)), dma((2, 3)), dma((2, 3)),
             dma((7,)), dma((7,)), dma((3,)), dma((3,)), dma((3,)), dma((3,)),
         ],
         compiler_params=pltpu.CompilerParams(

time: 53.6 us -> 52 us (0.970)
  Pallas kernels: 52.1 us -> 50.5 us
    pallas_call x1, Pallas kernels: 50.4 us -> 48.8 us  [on_device(): pl.pallas_call(kernel, out_shape=shapes, in_specs=[hbm] * 6, out_specs=(h...]
where the time goes in v4:
time: 52 us; the launch traced here: 51.8 us
  Pallas kernels  50.5 us (97%)
  between operations  1.29 us (2%)
    pallas_call x1, Pallas kernels, on_device(): pl.pallas_call(kernel, out_shape=shapes, in_specs=[hbm] * 6, out_specs=(h...  48.8 us
    pallas_call x1, Pallas kernels, on_device(): pl.pallas_call(hand_over, out_shape=shapes, in_specs=[hbm] * 4, out_specs...  1.7 us

profile of v4, /device:TPU:1, one launch (start us, length us, event | category | flops | bytes accessed | tf_op | source)
XLA Modules:
  0.0 51.8 jit_solution(14153568284576754005)
XLA Ops:
  1.3 48.8 %shard_map.93 = (bf16[256,256]{1,0:T(8,128)(2,1)}, bf16[256,256]{1,0:T(8,128)(2,1)}, f32[1,256]{1,0:T(1,128)}, f32[20,256]{1,0:T(8,128)}) custom-call(bf16[256,256]{1,0:T(8,128)(2,1)} %gate_hbm.1, bf16[256,256]{1,0:T(8,128)(2,1)} %up_hbm.1, bf16[256,3840]{1,0:T(8,128)(2,1)} %og_hbm.1, f32[1,256]{1,0:T(1,128)} %bitcast.4, s32[1,1]{1,0:T(1,128)} %bitcast.3.counts_hbm, ...), custom_call_target="tpu_custom_call" | custom-call | flops 1006632960 | bytes 3000000 | tf_op jit(solution)/shard_map/pallas_call | solution.py:283
  50.1 1.7 %shard_map.94 = (bf16[256,256]{1,0:T(8,128)(2,1)}, bf16[256,256]{1,0:T(8,128)(2,1)}, f32[1,256]{1,0:T(1,128)}, f32[20,256]{1,0:T(8,128)}) custom-call(bf16[256,256]{1,0:T(8,128)(2,1)} %get-tuple-element.12.a_in, bf16[256,256]{1,0:T(8,128)(2,1)} %get-tuple-element.13.b_in, f32[1,256]{1,0:T(1,128)} %get-tuple-element.14.c_in, f32[20,256]{1,0:T(8,128)} %get-tuple-element.15.d_in), custom_call_target="tpu_custom_call" | custom-call | tf_op jit(solution)/shard_map/pallas_call | solution.py:332
